TPU v7x, 256 devices: a whole 4x4x8 slice. The times are simulated.
256 devices in a mesh: lat: 8 (over y, x_lo), lon: 32 (over z, x_hi, core).
Axes of the slice: x: 4 (x_hi: 2, x_lo: 2; x = x_hi * 2 + x_lo), y: 4, z: 8, core: 2. Of those that a mesh axis runs over, the one named last changes fastest.
Arguments:
- tokens: bfloat16 [4, 144, 768, 512], P(None, 'lat', 'lon'), may hold values from -6 to 6
- lat_shift: int32 [1], replicated, may hold values from 1 to 5
- lon_shift: int32 [1], replicated, may hold values from 1 to 11
- lat_valid: int32 [144], replicated, may hold values from 0 to 1, as said below
- ln1_gain: float32 [512], replicated, may hold values from 0.1 to 1.9
- ln1_bias: float32 [512], replicated, may hold values from -3 to 3
- w_qkv: bfloat16 [512, 1536], replicated
- w_proj: bfloat16 [512, 512], replicated, may hold values from -0.25 to 0.25
- b_proj: float32 [512], replicated, may hold values from -3 to 3
- ln2_gain: float32 [512], replicated, may hold values from 0.1 to 1.9
- ln2_bias: float32 [512], replicated, may hold values from -3 to 3
- w_fc1: bfloat16 [512, 2048], replicated, may hold values from -0.25 to 0.25
- b_fc1: float32 [2048], replicated, may hold values from -3 to 3
- w_fc2: bfloat16 [2048, 512], replicated, may hold values from -0.125 to 0.125
- b_fc2: float32 [512], replicated, may hold values from -3 to 3
- merge_gain: float32 [2048], replicated, may hold values from 0.1 to 1.9
- merge_bias: float32 [2048], replicated, may hold values from -3 to 3
- w_merge: bfloat16 [2048, 1024], replicated, may hold values from -0.125 to 0.125
Outputs:
- merged: bfloat16 [4, 72, 384, 1024], P(None, 'lat', 'lon')
Inputs may be any that keep to these rules, and one draw needn't show every extreme that they name: lat_valid is 0 on the first 0 to 5 rows and on the last 1 to 18 rows of the grid, and 1 on every row between.
All inputs are finite; a program needn't handle non-finite values.
Results may differ from a plain program's by a relative error of at most 0.012.
Values may be sent and summed in bfloat16 or wider, within the bound.
A program may use at most 192 MiB of HBM per device.

v0:
```python
import functools

import jax
import jax.numpy as jnp
import numpy as np
from jax import lax
from jax.experimental import pallas as pl
from jax.experimental.pallas import tpu as pltpu
from jax.sharding import PartitionSpec as P

WIN_LAT = 6
WIN_LON = 12
UNIT = 144
HALF = 72
WIDTH = 512
FF = 2048
NORM_EPS = 1e-05
MESH = pl.DeviceIdType.MESH
BF16 = jnp.bfloat16
F32 = jnp.float32


def constants():
    rows = np.arange(UNIT)
    slot_i, slot_j = rows % HALF // WIN_LON, rows % WIN_LON
    block, within = rows // HALF, rows % HALF
    source = within // WIN_LON * 24 + block * WIN_LON + within % WIN_LON
    split = np.zeros((UNIT, UNIT), np.float32)
    split[rows, source] = 1.0
    gather = np.zeros((160, UNIT), np.float32)
    for part in range(4):
        col_odd, row_odd = part // 2, part % 2
        for row in range(3):
            for col in range(12):
                token = col // 6 * HALF + (2 * row + row_odd) * WIN_LON + 2 * (col % 6) + col_odd
                gather[part * 40 + row * 12 + col, token] = 1.0
    wide = np.ones((1, WIDTH), np.float32)
    grid = np.ones((UNIT, UNIT), np.float32)
    pairs = np.stack(
        (
            slot_i[:, None] * grid,
            slot_i[None, :] * grid,
            (rows[:, None] // HALF == rows[None, :] // HALF) * grid,
            np.eye(UNIT),
        )
    )
    return (
        jnp.asarray(split, BF16),
        jnp.asarray(gather, BF16),
        jnp.asarray(slot_i[:, None] * wide, BF16),
        jnp.asarray(slot_j[:, None] * wide, BF16),
        jnp.asarray(pairs, F32),
    )


def norm(values, gain, bias):
    mean = jnp.mean(values, axis=-1, keepdims=True)
    centred = values - mean
    var = jnp.mean(centred * centred, axis=-1, keepdims=True)
    return centred * lax.rsqrt(var + NORM_EPS) * gain + bias


def dot(left, right):
    return jnp.dot(left, right, preferred_element_type=F32)


def block_kernel(
    lats,
    lons,
    row_shift_ref,
    col_shift_ref,
    valid_ref,
    split_ref,
    gather_ref,
    slot_i_ref,
    slot_j_ref,
    pairs_ref,
    ln1_gain,
    ln1_bias,
    b_proj,
    ln2_gain,
    ln2_bias,
    b_fc1,
    b_fc2,
    merge_gain,
    merge_bias,
    x_hbm,
    w_qkv_hbm,
    w_proj_hbm,
    w_fc1_hbm,
    w_fc2_hbm,
    w_merge_hbm,
    out_ref,
    x_raw,
    w_qkv,
    w_proj,
    w_fc1,
    w_fc2,
    w_merge,
    tokens,
    normed,
    context,
    mixed,
    bias,
    qkv,
    grouped,
    x_sem,
    w_sem,
    in_lon_send,
    in_lon_recv,
    in_lat_send,
    in_lat_recv,
    in_diag_send,
    in_diag_recv,
    back_lon_send,
    back_lon_recv,
    back_lat_send,
    back_lat_recv,
    back_diag_send,
    back_diag_recv,
):
    lat, lon = lax.axis_index("lat"), lax.axis_index("lon")
    row_shift, col_shift = row_shift_ref[0], col_shift_ref[0]
    weights = [
        pltpu.make_async_copy(source, target, w_sem.at[place])
        for place, (source, target) in enumerate(
            (
                (w_qkv_hbm, w_qkv),
                (w_proj_hbm, w_proj),
                (w_fc1_hbm, w_fc1),
                (w_fc2_hbm, w_fc2),
                (w_merge_hbm, w_merge),
            )
        )
    ]

    def level_of(kind, half):
        return 1 + half + kind * (2 * half - 1)

    def x_copy(kind, half, band):
        level = level_of(kind, half)
        return pltpu.make_async_copy(
            x_hbm.at[level, band], x_raw.at[level, band], x_sem.at[level, band]
        )

    for step in range(3):
        for kind in range(2):
            for half in range(2):
                x_copy(kind, half, 2 - step if kind else step).start()
    for copy in weights:
        copy.start()

    def device(lat_step, lon_step):
        return {
            "lat": lax.rem(lat + lat_step + lats, lats),
            "lon": lax.rem(lon + lon_step + lons, lons),
        }

    def remote(ref, kind, source, target, send, recv, place):
        return pltpu.make_async_remote_copy(
            src_ref=ref.at[kind, source[0], source[1]],
            dst_ref=ref.at[kind, target[0], target[1]],
            send_sem=send,
            recv_sem=recv,
            device_id=place,
            device_id_type=MESH,
        )

    def in_lon(kind, band):
        return remote(
            normed,
            kind,
            (band + kind, 2 * kind),
            (band + kind, 2 - 2 * kind),
            in_lon_send.at[kind, band],
            in_lon_recv.at[kind, band],
            device(0, 2 * kind - 1),
        )

    def in_lat(kind, col):
        return remote(
            normed,
            kind,
            (3 * kind, col + kind),
            (3 - 3 * kind, col + kind),
            in_lat_send.at[kind, col],
            in_lat_recv.at[kind, col],
            device(2 * kind - 1, 0),
        )

    def in_diag(kind):
        return remote(
            normed,
            kind,
            (3 * kind, 2 * kind),
            (3 - 3 * kind, 2 - 2 * kind),
            in_diag_send.at[kind],
            in_diag_recv.at[kind],
            device(2 * kind - 1, 2 * kind - 1),
        )

    def back_lon(kind, band):
        return remote(
            context,
            kind,
            (band + 1 - kind, 2 - 2 * kind),
            (band + 1 - kind, 2 * kind),
            back_lon_send.at[kind, band],
            back_lon_recv.at[kind, band],
            device(0, 1 - 2 * kind),
        )

    def back_lat(kind, col):
        return remote(
            context,
            kind,
            (3 - 3 * kind, col + 1 - kind),
            (3 * kind, col + 1 - kind),
            back_lat_send.at[kind, col],
            back_lat_recv.at[kind, col],
            device(1 - 2 * kind, 0),
        )

    def back_diag(kind):
        return remote(
            context,
            kind,
            (3 - 3 * kind, 2 - 2 * kind),
            (3 * kind, 2 * kind),
            back_diag_send.at[kind],
            back_diag_recv.at[kind],
            device(1 - 2 * kind, 1 - 2 * kind),
        )

    barrier = pltpu.get_barrier_semaphore()
    for lat_step, lon_step in ((0, 1), (0, -1), (1, 0), (-1, 0), (1, 1), (-1, -1)):
        pl.semaphore_signal(
            barrier, inc=1, device_id=device(lat_step, lon_step), device_id_type=MESH
        )

    def prepare(kind, band):
        parts = []
        for half in range(2):
            x_copy(kind, half, band).wait()
            raw = x_raw[level_of(kind, half), band]
            scaled = norm(raw.astype(F32), ln1_gain[...], ln1_bias[...]).astype(BF16)
            parts.append(dot(split_ref[...], jnp.concatenate((raw, scaled), axis=1)))
        for col in range(2):
            rows = slice(col * HALF, (col + 1) * HALF)
            block = jnp.concatenate((parts[0][rows], parts[1][rows]), axis=0).astype(BF16)
            tokens[kind, band, col] = block[:, :WIDTH]
            normed[kind, band + kind, col + kind] = block[:, WIDTH:]

    def prepare_edge(kind, carry):
        prepare(kind, 2 * kind)
        return carry

    def prepare_rest(step, carry):
        kind, place = step % 2, 1 + step // 2
        band = place + kind * (2 - 2 * place)
        prepare(kind, band)
        in_lon(kind, band).start()
        return carry

    lax.fori_loop(0, 2, prepare_edge, 0)
    pl.semaphore_wait(barrier, 6)
    for kind in range(2):
        in_lon(kind, 2 * kind).start()
        in_diag(kind).start()
        in_lat(kind, 0).start()
        in_lat(kind, 1).start()
    lax.fori_loop(0, 4, prepare_rest, 0)

    def allow(step, carry):
        kind, band = step % 2, step // 2
        first = lat * 3 * WIN_LAT + (band - kind) * WIN_LAT + lats * 3 * WIN_LAT
        usable = jnp.zeros((UNIT, UNIT), F32)
        for slot in range(WIN_LAT):
            row = first + slot + jnp.where(slot < row_shift, WIN_LAT, 0)
            value = valid_ref[lax.rem(row, lats * 3 * WIN_LAT)].astype(F32)
            usable = jnp.where(pairs_ref[1] == slot, value, usable)
        seam = jnp.where(kind == 0, (lat == lats - 1) & (band == 2), (lat == 0) & (band == 0))
        shift = row_shift.astype(F32)
        query_side = jnp.where(pairs_ref[0] < shift, 1.0, 0.0)
        key_side = jnp.where(pairs_ref[1] < shift, 1.0, 0.0)
        apart = jnp.abs(query_side - key_side) * jnp.where(seam, 1.0, 0.0)
        apart = apart + (1.0 - pairs_ref[2]) * jnp.where(kind == 0, 0.0, 1.0)
        serves = (apart < 0.5) & (jnp.maximum(usable, pairs_ref[3]) > 0.5)
        bias[kind, band] = jnp.where(serves, 0.0, -jnp.inf)
        return carry

    lax.fori_loop(0, 6, allow, 0)
    weights[0].wait()

    row_bf, col_bf = row_shift.astype(F32).astype(BF16), col_shift.astype(F32).astype(BF16)

    def pick(ref, kind, band, col, below):
        low_i, low_j = slot_i_ref[...] < row_bf, slot_j_ref[...] < col_bf
        near, far = (1, 0) if below else (0, 1)
        top = jnp.where(low_j, ref[kind, band + near, col + near], ref[kind, band + near, col + far])
        bottom = jnp.where(low_j, ref[kind, band + far, col + near], ref[kind, band + far, col + far])
        return jnp.where(low_i, top, bottom)

    lane = lax.broadcasted_iota(jnp.int32, (UNIT, 128), 1)

    def attend(stage):
        def body(kind, carry):
            places = []
            for item in range(2):
                band, col = ((item, 0), (item, 1), (2, item))[stage]
                places.append((band + kind * (2 - 2 * band), col + kind * (1 - 2 * col)))
            window = jnp.concatenate(
                [pick(normed, kind, band, col, True) for band, col in places], axis=0
            )
            for part in range(3):
                columns = slice(part * WIDTH, (part + 1) * WIDTH)
                value = dot(window, w_qkv[:, columns])
                qkv[:, columns] = (value * 0.125 if part == 0 else value).astype(BF16)
            for item, (band, col) in enumerate(places):
                rows = slice(item * UNIT, (item + 1) * UNIT)
                for pair in range(4):
                    columns = slice(pair * 128, (pair + 1) * 128)
                    query = qkv[rows, columns].astype(F32)
                    query = jnp.concatenate(
                        (jnp.where(lane < 64, query, 0.0), jnp.where(lane < 64, 0.0, query)), axis=0
                    ).astype(BF16)
                    key = qkv[rows, WIDTH + pair * 128 : WIDTH + (pair + 1) * 128]
                    value = qkv[rows, 2 * WIDTH + pair * 128 : 2 * WIDTH + (pair + 1) * 128]
                    scores = lax.dot_general(
                        query, key, (((1,), (1,)), ((), ())), preferred_element_type=F32
                    )
                    mask = bias[kind, band]
                    scores = scores + jnp.concatenate((mask, mask), axis=0)
                    top = jnp.max(scores, axis=-1, keepdims=True)
                    share = jnp.exp(scores - top).astype(BF16)
                    value = jnp.concatenate((value, jnp.ones((UNIT, 128), BF16)), axis=1)
                    total = dot(share, value)
                    total = total[:, :128] / total[:, 128:]
                    context[kind, band + 1 - kind, col + 1 - kind, :, columns] = jnp.where(
                        lane < 64, total[:UNIT], total[UNIT:]
                    ).astype(BF16)
            return carry

        lax.fori_loop(0, 2, body, 0)

    attend(0)
    for kind in range(2):
        for band in range(3):
            in_lon(kind, band).wait_recv()
    attend(1)
    for kind in range(2):
        back_lon(kind, kind).start()
        back_lon(kind, 1 + kind).start()
    for kind in range(2):
        in_lat(kind, 0).wait_recv()
        in_lat(kind, 1).wait_recv()
        in_diag(kind).wait_recv()
    attend(2)
    for kind in range(2):
        back_lon(kind, 2 - 2 * kind).start()
        back_diag(kind).start()
        back_lat(kind, 0).start()
        back_lat(kind, 1).start()
    for copy in weights[1:4]:
        copy.wait()

    def finish(stage):
        def body(kind, carry):
            places = []
            for item in range(2):
                band, col = ((1 + item, 1), (1 + item, 0), (0, item))[stage]
                places.append((band + kind * (2 - 2 * band), col + kind * (1 - 2 * col)))
            attended = jnp.concatenate(
                [pick(context, kind, band, col, False) for band, col in places], axis=0
            )
            base = jnp.concatenate([tokens[kind, band, col] for band, col in places], axis=0)
            residual = base.astype(F32) + dot(attended, w_proj[...]) + b_proj[...]
            residual = residual.astype(BF16).astype(F32)
            scaled = norm(residual, ln2_gain[...], ln2_bias[...]).astype(BF16)
            total = residual + b_fc2[...]
            for part in range(4):
                columns = slice(part * WIDTH, (part + 1) * WIDTH)
                inner = dot(scaled, w_fc1[:, columns]) + b_fc1[:, columns]
                hidden = 0.5 * inner * (1.0 + lax.erf(inner * np.float32(0.5**0.5)))
                total = total + dot(hidden.astype(BF16), w_fc2[columns, :])
            total = total.astype(BF16).astype(F32)
            for item, (band, col) in enumerate(places):
                mixed[kind, band, col] = total[item * UNIT : (item + 1) * UNIT]
            return carry

        lax.fori_loop(0, 2, body, 0)

    finish(0)
    for kind in range(2):
        for band in range(3):
            back_lon(kind, band).wait_recv()
    finish(1)
    for kind in range(2):
        back_lat(kind, 0).wait_recv()
        back_lat(kind, 1).wait_recv()
        back_diag(kind).wait_recv()
    finish(2)

    def group(step, carry):
        kind, band = step % 2, step // 2
        for half in range(2):
            rows = slice(half * HALF, (half + 1) * HALF)
            level = jnp.concatenate((mixed[kind, band, 0, rows], mixed[kind, band, 1, rows]), axis=0)
            parts = dot(gather_ref[...], level.astype(BF16))
            parts = jnp.concatenate([parts[40 * part : 40 * part + 40] for part in range(4)], axis=1)
            grouped[step, half * 40 : half * 40 + 40] = norm(parts, merge_gain[...], merge_bias[...])
        return carry

    lax.fori_loop(0, 6, group, 0)
    weights[4].wait()
    for part in range(4):
        columns = slice(part * 256, (part + 1) * 256)
        merged = dot(
            grouped[...].reshape(480, FF).astype(BF16), w_merge[:, columns]
        )
        for step in range(6):
            kind, band = step % 2, step // 2
            for half in range(2):
                for row in range(3):
                    first = step * 80 + half * 40 + row * 12
                    out_ref[level_of(kind, half), band * 3 + row, :, columns] = merged[
                        first : first + 12
                    ].astype(BF16)

    for kind in range(2):
        for band in range(3):
            in_lon(kind, band).wait_send()
            back_lon(kind, band).wait_send()
        for col in range(2):
            in_lat(kind, col).wait_send()
            back_lat(kind, col).wait_send()
        in_diag(kind).wait_send()
        back_diag(kind).wait_send()


def solution(mesh):
    lats, lons = mesh.shape["lat"], mesh.shape["lon"]

    def on_device(
        tokens,
        lat_shift,
        lon_shift,
        lat_valid,
        ln1_gain,
        ln1_bias,
        w_qkv,
        w_proj,
        b_proj,
        ln2_gain,
        ln2_bias,
        w_fc1,
        b_fc1,
        w_fc2,
        b_fc2,
        merge_gain,
        merge_bias,
        w_merge,
    ):
        smem = pl.BlockSpec(memory_space=pltpu.SMEM)
        vmem = pl.BlockSpec(memory_space=pltpu.VMEM)
        hbm = pl.BlockSpec(memory_space=pl.ANY)
        dma = pltpu.SemaphoreType.DMA
        vectors = (
            ln1_gain,
            ln1_bias,
            b_proj,
            ln2_gain,
            ln2_bias,
            b_fc1,
            b_fc2,
            merge_gain,
            merge_bias,
        )
        return pl.pallas_call(
            functools.partial(block_kernel, lats, lons),
            out_shape=jax.ShapeDtypeStruct((4, 9, 12, 1024), BF16),
            in_specs=[smem] * 3 + [vmem] * 14 + [hbm] * 6,
            out_specs=vmem,
            scratch_shapes=[
                pltpu.VMEM((4, 3, UNIT, WIDTH), BF16),
                pltpu.VMEM((WIDTH, 3 * WIDTH), BF16),
                pltpu.VMEM((WIDTH, WIDTH), BF16),
                pltpu.VMEM((WIDTH, FF), BF16),
                pltpu.VMEM((FF, WIDTH), BF16),
                pltpu.VMEM((FF, 1024), BF16),
                pltpu.VMEM((2, 3, 2, UNIT, WIDTH), BF16),
                pltpu.VMEM((2, 4, 3, UNIT, WIDTH), BF16),
                pltpu.VMEM((2, 4, 3, UNIT, WIDTH), BF16),
                pltpu.VMEM((2, 3, 2, UNIT, WIDTH), F32),
                pltpu.VMEM((2, 3, UNIT, UNIT), F32),
                pltpu.VMEM((2 * UNIT, 3 * WIDTH), BF16),
                pltpu.VMEM((6, 80, FF), F32),
                dma((4, 3)),
                dma((5,)),
            ]
            + [dma((2, 3))] * 2
            + [dma((2, 2))] * 2
            + [dma((2,))] * 2
            + [dma((2, 3))] * 2
            + [dma((2, 2))] * 2
            + [dma((2,))] * 2,
            compiler_params=pltpu.CompilerParams(
                collective_id=0, has_side_effects=True, vmem_limit_bytes=58 * 1024 * 1024
            ),
        )(
            lat_shift,
            lon_shift,
            lat_valid,
            *constants(),
            *(vector.reshape(1, -1) for vector in vectors),
            tokens.reshape(4, 3, UNIT, WIDTH),
            w_qkv,
            w_proj,
            w_fc1,
            w_fc2,
            w_merge,
        )

    return jax.shard_map(
        on_device,
        mesh=mesh,
        in_specs=(P(None, "lat", "lon", None),) + (P(),) * 17,
        out_specs=P(None, "lat", "lon", None),
        check_vma=False,
    )
```

profile of v0, /device:TPU:1, one launch (start us, length us, event | category | flops | bytes accessed | tf_op | source)
XLA Modules:
  0.0 79.8 jit_solution(10088017223042633420)
XLA Ops:
  1.3 75.6 %shard_map.217 = bf16[4,9,12,1024]{3,2,1,0:T(8,128)(2,1)} custom-call(s32[1]{0:T(128)S(6)} %copy.25.row_shift_ref, s32[1]{0:T(128)S(6)} %copy.26.col_shift_ref, s32[144]{0:T(256)} %valid_ref.1, bf16[144,144]{1,0:T(8,128)(2,1)} %constant.10.clone.split_ref, bf16[160,144]{1,0:T(8,128)(2,1)} %constant.11.clone.gather_ref, ...), custom_call_target="tpu_custom_call" | custom-call | tf_op jit(solution)/shard_map/pallas_call | solution.py:479
  76.9 2.9 %copy.24 = bf16[4,9,12,1024]{3,0,2,1:T(4,128)(2,1)} copy(bf16[4,9,12,1024]{3,2,1,0:T(8,128)(2,1)} %shard_map.217) | data formatting | bytes 1769472 | tf_op jit(solution)/shard_map/pallas_call | solution.py:479
where the time goes:
time: 79.9 us; the launch traced here: 79.8 us
  Pallas kernels  75.6 us (95%)
  local copies, waits for them, and re-layouts  2.88 us (4%)
  between operations  1.31 us (2%)
    pallas_call x1, Pallas kernels, on_device(): pl.pallas_call(functools.partial(block_kernel, lats, lons), out_shape=jax...  75.6 us
    pallas_call x1, local copies, waits for them, and re-layouts, on_device(): pl.pallas_call(functools.partial(block_kernel, lats, lons), out_shape=jax...  2.88 us

commit v1 on v0

v1 whole, which is shorter than its diff:
```python
import functools

import jax
import jax.numpy as jnp
import numpy as np
from jax import lax
from jax.experimental import pallas as pl
from jax.experimental.pallas import tpu as pltpu
from jax.sharding import PartitionSpec as P

WIN_LAT = 6
WIN_LON = 12
UNIT = 144
HALF = 72
WIDTH = 512
FF = 2048
NORM_EPS = 1e-05
MESH = pl.DeviceIdType.MESH
BF16 = jnp.bfloat16
F32 = jnp.float32


def constants():
    rows = np.arange(UNIT)
    block, within = rows // HALF, rows % HALF
    source = within // WIN_LON * 24 + block * WIN_LON + within % WIN_LON
    split = np.zeros((UNIT, UNIT), np.float32)
    split[rows, source] = 1.0
    gather = np.zeros((192, 192), np.float32)
    for part in range(4):
        col_odd, row_odd = part // 2, part % 2
        for col in range(12):
            for level in range(4):
                kind, half = (1, level // 3) if level in (0, 3) else (0, level - 1)
                token = kind * 96 + col // 6 * 48 + row_odd * 24 + half * 12 + 2 * (col % 6) + col_odd
                gather[part * 48 + col * 4 + level, token] = 1.0
    slot_i, slot_j = rows // 24, rows % WIN_LON
    half = rows // WIN_LON % 2
    wide = np.ones((1, WIDTH), np.float32)
    grid = np.ones((UNIT, UNIT), np.float32)
    pairs = np.stack(
        (
            slot_i[:, None] * grid,
            slot_i[None, :] * grid,
            (half[:, None] == half[None, :]) * grid,
            np.eye(UNIT),
        )
    )
    return (
        jnp.asarray(split, BF16),
        jnp.asarray(gather, BF16),
        jnp.asarray(slot_i[:, None] * wide, BF16),
        jnp.asarray(slot_j[:, None] * wide, BF16),
        jnp.asarray(pairs, F32),
    )


def norm(values, gain, bias):
    mean = jnp.mean(values, axis=-1, keepdims=True)
    centred = values - mean
    var = jnp.mean(centred * centred, axis=-1, keepdims=True)
    return centred * lax.rsqrt(var + NORM_EPS) * gain + bias


def dot(left, right):
    return jnp.dot(left, right, preferred_element_type=F32)


def block_kernel(
    lats,
    lons,
    row_shift,
    col_shift_ref,
    valid_ref,
    split_ref,
    gather_ref,
    slot_i_ref,
    slot_j_ref,
    pairs_ref,
    ln1_gain,
    ln1_bias,
    b_proj,
    ln2_gain,
    ln2_bias,
    b_fc1,
    b_fc2,
    merge_gain,
    merge_bias,
    x_hbm,
    w_qkv_hbm,
    w_proj_hbm,
    w_fc1_hbm,
    w_fc2_hbm,
    w_merge_hbm,
    out_ref,
    x_raw,
    w_qkv,
    w_proj,
    w_fc1,
    w_fc2,
    w_merge,
    tokens,
    normed,
    context,
    mixed,
    bias,
    qkv,
    grouped,
    x_sem,
    w_sem,
    in_lon_send,
    in_lon_recv,
    in_lat_send,
    in_lat_recv,
    in_diag_send,
    in_diag_recv,
    back_lon_send,
    back_lon_recv,
    back_lat_send,
    back_lat_recv,
    back_diag_send,
    back_diag_recv,
):
    lat, lon = lax.axis_index("lat"), lax.axis_index("lon")
    col_shift = col_shift_ref[0]
    side = 0 if row_shift <= 3 else 1
    count = {1: 32, 2: 48, 3: 80}[row_shift if side == 0 else WIN_LAT - row_shift]
    crossing = pl.ds(side * (UNIT - count), count)
    weights = [
        pltpu.make_async_copy(source, target, w_sem.at[place])
        for place, (source, target) in enumerate(
            (
                (w_qkv_hbm, w_qkv),
                (w_proj_hbm, w_proj),
                (w_fc1_hbm, w_fc1),
                (w_fc2_hbm, w_fc2),
                (w_merge_hbm, w_merge),
            )
        )
    ]

    def level_of(kind, half):
        return 1 + half + kind * (2 * half - 1)

    def x_copy(kind, half, band):
        level = level_of(kind, half)
        return pltpu.make_async_copy(
            x_hbm.at[level, band], x_raw.at[level, band], x_sem.at[level, band]
        )

    for band in range(3):
        for kind in range(2):
            for half in range(2):
                x_copy(kind, half, band).start()
    for copy in weights:
        copy.start()

    def device(lat_step, lon_step):
        return {
            "lat": lax.rem(lat + lat_step + lats, lats),
            "lon": lax.rem(lon + lon_step + lons, lons),
        }

    def remote(ref, kind, source, target, send, recv, place, rows=pl.ds(0, UNIT)):
        return pltpu.make_async_remote_copy(
            src_ref=ref.at[kind, source[0], source[1], rows],
            dst_ref=ref.at[kind, target[0], target[1], rows],
            send_sem=send,
            recv_sem=recv,
            device_id=place,
            device_id_type=MESH,
        )

    def in_lon(kind, band):
        return remote(
            normed,
            kind,
            (band + side, 2 * kind),
            (band + side, 2 - 2 * kind),
            in_lon_send.at[kind, band],
            in_lon_recv.at[kind, band],
            device(0, 2 * kind - 1),
        )

    def in_lat(kind, col):
        return remote(
            normed,
            kind,
            (3 * side, col + kind),
            (3 - 3 * side, col + kind),
            in_lat_send.at[kind, col],
            in_lat_recv.at[kind, col],
            device(2 * side - 1, 0),
            crossing,
        )

    def in_diag(kind):
        return remote(
            normed,
            kind,
            (3 * side, 2 * kind),
            (3 - 3 * side, 2 - 2 * kind),
            in_diag_send.at[kind],
            in_diag_recv.at[kind],
            device(2 * side - 1, 2 * kind - 1),
            crossing,
        )

    def back_lon(kind, band):
        return remote(
            context,
            kind,
            (band + 1 - side, 2 - 2 * kind),
            (band + 1 - side, 2 * kind),
            back_lon_send.at[kind, band],
            back_lon_recv.at[kind, band],
            device(0, 1 - 2 * kind),
        )

    def back_lat(kind, col):
        return remote(
            context,
            kind,
            (3 - 3 * side, col + 1 - kind),
            (3 * side, col + 1 - kind),
            back_lat_send.at[kind, col],
            back_lat_recv.at[kind, col],
            device(1 - 2 * side, 0),
            crossing,
        )

    def back_diag(kind):
        return remote(
            context,
            kind,
            (3 - 3 * side, 2 - 2 * kind),
            (3 * side, 2 * kind),
            back_diag_send.at[kind],
            back_diag_recv.at[kind],
            device(1 - 2 * side, 1 - 2 * kind),
            crossing,
        )

    neighbours = [(0, 1), (0, -1)] + [(a, b) for a in (1, -1) for b in (0, 1, -1)]
    barrier = pltpu.get_barrier_semaphore()
    for lat_step, lon_step in neighbours:
        pl.semaphore_signal(
            barrier, inc=1, device_id=device(lat_step, lon_step), device_id_type=MESH
        )

    def prepare(step, carry):
        kind, band = step % 2, step // 2
        raws, norms = [], []
        for half in range(2):
            x_copy(kind, half, band).wait()
            raw = x_raw[level_of(kind, half), band].astype(F32)
            raws.append(raw)
            norms.append(norm(raw, ln1_gain[...], ln1_bias[...]))
        parts = []
        for third in range(2):
            rows = [slice(24 * i, 24 * i + 24) for i in range(3 * third, 3 * third + 3)]
            mixed_rows = [
                jnp.concatenate([level[row] for row in rows for level in levels], axis=0)
                for levels in (raws, norms)
            ]
            parts.append(dot(split_ref[...], jnp.concatenate(mixed_rows, axis=1).astype(BF16)))
        for col in range(2):
            rows = slice(col * HALF, (col + 1) * HALF)
            block = jnp.concatenate((parts[0][rows], parts[1][rows]), axis=0).astype(BF16)
            tokens[kind, band, col] = block[:, :WIDTH]
            normed[kind, band + side, col + kind] = block[:, WIDTH:]

        @pl.when(step == 0)
        def _():
            pl.semaphore_wait(barrier, len(neighbours))

        in_lon(kind, band).start()
        return carry

    lax.fori_loop(0, 6, prepare, 0)
    for kind in range(2):
        in_diag(kind).start()
        in_lat(kind, 0).start()
        in_lat(kind, 1).start()

    def allow(step, carry):
        kind, band = step % 2, step // 2
        first = lat * 3 * WIN_LAT + (band - side) * WIN_LAT + lats * 3 * WIN_LAT
        usable = jnp.zeros((UNIT, UNIT), F32)
        for slot in range(WIN_LAT):
            row = first + slot + (WIN_LAT if slot < row_shift else 0)
            value = valid_ref[lax.rem(row, lats * 3 * WIN_LAT)].astype(F32)
            usable = jnp.where(pairs_ref[1] == slot, value, usable)
        seam = (lat == 0) & (band == 0) if side else (lat == lats - 1) & (band == 2)
        query_side = jnp.where(pairs_ref[0] < row_shift, 1.0, 0.0)
        key_side = jnp.where(pairs_ref[1] < row_shift, 1.0, 0.0)
        apart = jnp.abs(query_side - key_side) * jnp.where(seam, 1.0, 0.0)
        apart = apart + (1.0 - pairs_ref[2]) * jnp.where(kind == 0, 0.0, 1.0)
        serves = (apart < 0.5) & (jnp.maximum(usable, pairs_ref[3]) > 0.5)
        bias[kind, band] = jnp.where(serves, 0.0, -jnp.inf)
        return carry

    lax.fori_loop(0, 6, allow, 0)
    weights[0].wait()

    col_bf = col_shift.astype(F32).astype(BF16)

    def pick(ref, kind, band, col, below):
        low_i, low_j = slot_i_ref[...] < BF16(row_shift), slot_j_ref[...] < col_bf
        near, far = (1, 0) if below else (0, 1)
        top = jnp.where(low_j, ref[kind, band + near, col + near], ref[kind, band + near, col + far])
        bottom = jnp.where(low_j, ref[kind, band + far, col + near], ref[kind, band + far, col + far])
        return jnp.where(low_i, top, bottom)

    lane = lax.broadcasted_iota(jnp.int32, (UNIT, 128), 1)

    def places_of(kind, rows, cols):
        return [
            (2 - row if side else row, col + kind * (1 - 2 * col)) for row, col in zip(rows, cols)
        ]

    def attend(step, carry):
        kind, stage = step % 2, step // 2
        last = stage // 2

        @pl.when(stage == 1)
        def _():
            for band in range(3):
                in_lon(kind, band).wait_recv()

        @pl.when(stage == 2)
        def _():
            in_lat(kind, 0).wait_recv()
            in_lat(kind, 1).wait_recv()
            in_diag(kind).wait_recv()

        places = places_of(
            kind,
            [item + last * (2 - item) for item in range(2)],
            [stage * (1 - last) + last * item for item in range(2)],
        )
        window = jnp.concatenate(
            [pick(normed, kind, band, col, True) for band, col in places], axis=0
        )
        for part in range(3):
            columns = slice(part * WIDTH, (part + 1) * WIDTH)
            value = dot(window, w_qkv[:, columns])
            qkv[:, columns] = (value * 0.125 if part == 0 else value).astype(BF16)
        for item, (band, col) in enumerate(places):
            rows = slice(item * UNIT, (item + 1) * UNIT)
            for pair in range(4):
                columns = slice(pair * 128, (pair + 1) * 128)
                query = qkv[rows, columns].astype(F32)
                query = jnp.concatenate(
                    (jnp.where(lane < 64, query, 0.0), jnp.where(lane < 64, 0.0, query)), axis=0
                ).astype(BF16)
                key = qkv[rows, WIDTH + pair * 128 : WIDTH + (pair + 1) * 128]
                value = qkv[rows, 2 * WIDTH + pair * 128 : 2 * WIDTH + (pair + 1) * 128]
                scores = lax.dot_general(
                    query, key, (((1,), (1,)), ((), ())), preferred_element_type=F32
                )
                mask = bias[kind, band]
                scores = scores + jnp.concatenate((mask, mask), axis=0)
                top = jnp.max(scores, axis=-1, keepdims=True)
                share = jnp.exp(scores - top).astype(BF16)
                value = jnp.concatenate((value, jnp.ones((UNIT, 128), BF16)), axis=1)
                total = dot(share, value)
                total = total[:, :128] / total[:, 128:]
                context[kind, band + 1 - side, col + 1 - kind, :, columns] = jnp.where(
                    lane < 64, total[:UNIT], total[UNIT:]
                ).astype(BF16)

        @pl.when(stage == 1)
        def _():
            for band, _ in places:
                back_lon(kind, band).start()

        @pl.when(stage == 2)
        def _():
            back_lon(kind, 2 - 2 * side).start()
            back_diag(kind).start()
            back_lat(kind, 0).start()
            back_lat(kind, 1).start()

        return carry

    lax.fori_loop(0, 6, attend, 0)
    for copy in weights[1:4]:
        copy.wait()

    def finish(step, carry):
        kind, stage = step % 2, step // 2
        last = stage // 2

        @pl.when(stage == 1)
        def _():
            for band in range(3):
                back_lon(kind, band).wait_recv()

        @pl.when(stage == 2)
        def _():
            back_lat(kind, 0).wait_recv()
            back_lat(kind, 1).wait_recv()
            back_diag(kind).wait_recv()

        places = places_of(
            kind,
            [(1 + item) * (1 - last) for item in range(2)],
            [(1 - stage) * (1 - last) + last * item for item in range(2)],
        )
        attended = jnp.concatenate(
            [pick(context, kind, band, col, False) for band, col in places], axis=0
        )
        base = jnp.concatenate([tokens[kind, band, col] for band, col in places], axis=0)
        residual = base.astype(F32) + dot(attended, w_proj[...]) + b_proj[...]
        residual = residual.astype(BF16).astype(F32)
        scaled = norm(residual, ln2_gain[...], ln2_bias[...]).astype(BF16)
        total = residual + b_fc2[...]
        for part in range(4):
            columns = slice(part * WIDTH, (part + 1) * WIDTH)
            inner = dot(scaled, w_fc1[:, columns]) + b_fc1[:, columns]
            hidden = 0.5 * inner * (1.0 + lax.erf(inner * np.float32(0.5**0.5)))
            total = total + dot(hidden.astype(BF16), w_fc2[columns, :])
        total = total.astype(BF16).astype(F32)
        for item, (band, col) in enumerate(places):
            mixed[kind, band, col] = total[item * UNIT : (item + 1) * UNIT]
        return carry

    lax.fori_loop(0, 6, finish, 0)

    def group(step, carry):
        band = step // 3
        rows = pl.ds(pl.multiple_of(step % 3 * 48, 48), 48)
        level = [mixed[kind, band, col, rows] for kind in range(2) for col in range(2)]
        parts = dot(gather_ref[...], jnp.concatenate(level, axis=0).astype(BF16))
        parts = jnp.concatenate([parts[48 * part : 48 * part + 48] for part in range(4)], axis=1)
        grouped[step] = norm(parts, merge_gain[...], merge_bias[...]).astype(BF16)
        return carry

    lax.fori_loop(0, 9, group, 0)
    weights[4].wait()
    for part in range(4):
        columns = slice(part * 256, (part + 1) * 256)
        merged = dot(grouped[...].reshape(432, FF), w_merge[:, columns])
        out_ref[:, columns] = merged.astype(BF16)

    for kind in range(2):
        for band in range(3):
            in_lon(kind, band).wait_send()
            back_lon(kind, band).wait_send()
        for col in range(2):
            in_lat(kind, col).wait_send()
            back_lat(kind, col).wait_send()
        in_diag(kind).wait_send()
        back_diag(kind).wait_send()


def solution(mesh):
    lats, lons = mesh.shape["lat"], mesh.shape["lon"]

    def on_device(
        tokens,
        lat_shift,
        lon_shift,
        lat_valid,
        ln1_gain,
        ln1_bias,
        w_qkv,
        w_proj,
        b_proj,
        ln2_gain,
        ln2_bias,
        w_fc1,
        b_fc1,
        w_fc2,
        b_fc2,
        merge_gain,
        merge_bias,
        w_merge,
    ):
        smem = pl.BlockSpec(memory_space=pltpu.SMEM)
        vmem = pl.BlockSpec(memory_space=pltpu.VMEM)
        hbm = pl.BlockSpec(memory_space=pl.ANY)
        dma = pltpu.SemaphoreType.DMA
        vectors = (
            ln1_gain,
            ln1_bias,
            b_proj,
            ln2_gain,
            ln2_bias,
            b_fc1,
            b_fc2,
            merge_gain,
            merge_bias,
        )
        def variant(row_shift, *operands):
            return pl.pallas_call(
                functools.partial(block_kernel, lats, lons, row_shift),
                out_shape=jax.ShapeDtypeStruct((432, 1024), BF16),
                in_specs=[smem] * 2 + [vmem] * 14 + [hbm] * 6,
                out_specs=vmem,
                scratch_shapes=[
                    pltpu.VMEM((4, 3, UNIT, WIDTH), BF16),
                    pltpu.VMEM((WIDTH, 3 * WIDTH), BF16),
                    pltpu.VMEM((WIDTH, WIDTH), BF16),
                    pltpu.VMEM((WIDTH, FF), BF16),
                    pltpu.VMEM((FF, WIDTH), BF16),
                    pltpu.VMEM((FF, 1024), BF16),
                    pltpu.VMEM((2, 3, 2, UNIT, WIDTH), BF16),
                    pltpu.VMEM((2, 4, 3, UNIT, WIDTH), BF16),
                    pltpu.VMEM((2, 4, 3, UNIT, WIDTH), BF16),
                    pltpu.VMEM((2, 3, 2, UNIT, WIDTH), F32),
                    pltpu.VMEM((2, 3, UNIT, UNIT), F32),
                    pltpu.VMEM((2 * UNIT, 3 * WIDTH), BF16),
                    pltpu.VMEM((9, 48, FF), BF16),
                    dma((4, 3)),
                    dma((5,)),
                ]
                + [dma((2, 3))] * 2
                + [dma((2, 2))] * 2
                + [dma((2,))] * 2
                + [dma((2, 3))] * 2
                + [dma((2, 2))] * 2
                + [dma((2,))] * 2,
                compiler_params=pltpu.CompilerParams(
                    collective_id=row_shift, has_side_effects=True, vmem_limit_bytes=58 * 1024 * 1024
                ),
            )(*operands)

        merged = lax.switch(
            lat_shift[0] - 1,
            [functools.partial(variant, row_shift) for row_shift in range(1, WIN_LAT)],
            lon_shift,
            lat_valid,
            *constants(),
            *(vector.reshape(1, -1) for vector in vectors),
            tokens.reshape(4, 3, UNIT, WIDTH),
            w_qkv,
            w_proj,
            w_fc1,
            w_fc2,
            w_merge,
        )
        return merged.reshape(9, 12, 4, 1024).transpose(2, 0, 1, 3)

    return jax.shard_map(
        on_device,
        mesh=mesh,
        in_specs=(P(None, "lat", "lon", None),) + (P(),) * 17,
        out_specs=P(None, "lat", "lon", None),
        check_vma=False,
    )
```

time: 79.9 us -> 58.4 us (0.73)
  the two profiles are of different devices: /device:TPU:1 before, /device:TPU:225 now
where the time goes in v1:
time: 58.4 us; the launch traced here: 58.2 us
  Pallas kernels  56.1 us (96%)
  local copies, waits for them, and re-layouts  1.23 us (2%)
  between operations  0.66 us (1%)
    pallas_call x1, Pallas kernels, variant(): pl.pallas_call(functools.partial(block_kernel, lats, lons, row_shift), ou...  56.1 us
    reshape x1, local copies, waits for them, and re-layouts, on_device(): return merged.reshape(9, 12, 4, 1024).transpose(2, 0, 1, 3)  1.23 us

profile of v1, /device:TPU:225, one launch (start us, length us, event | category | flops | bytes accessed | tf_op | source)
XLA Modules:
  0.0 58.2 jit_solution(14608172985240105618)
XLA Ops:
  0.7 56.4 %conditional.1 = (bf16[432,1024]{1,0:T(8,128)(2,1)S(1)}) conditional(s32[]{:T(128)} %bitcast, (s32[1]{0:T(128)}, s32[144]{0:T(256)}, bf16[144,144]{1,0:T(8,128)(2,1)}, bf16[192,192]{1,0:T(8,128)(2,1)}, bf16[144,512]{1,0:T(8,128)(2,1)}, /*index=5*/bf16[144,512]{1,0:T(8,128)(2,1)}, f32[4,144,144]{2,1,0:T(8,128)}, ...), branch_computations={%region_0.0_spmd, %region_1.0_spmd, %region_2.0_spmd, %region_3.0_... | conditional | bytes 8 | solution.py:530
  0.7 56.1 %branch_1_fun.1 = bf16[432,1024]{1,0:T(8,128)(2,1)S(1)} custom-call(s32[1]{0:T(128)} %get-tuple-element.253.col_shift_ref, s32[144]{0:T(256)} %get-tuple-element.254.valid_ref, bf16[144,144]{1,0:T(8,128)(2,1)} %get-tuple-element.255.split_ref, bf16[192,192]{1,0:T(8,128)(2,1)} %get-tuple-element.256.gather_ref, ...), custom_call_target="tpu_custom_call" | custom-call | tf_op jit(solution)/shard_map/cond/branch_1_fun/pallas_call | solution.py:497
  57.0 1.2 %reshape.48 = bf16[9,12,4,1024]{3,2,1,0:T(4,128)(2,1)} reshape(bf16[432,1024]{1,0:T(8,128)(2,1)S(1)} %get-tuple-element.341) | data formatting | bytes 1769472 | tf_op jit(solution)/shard_map/reshape | solution.py:544
